TPU v7x, 512 devices: a whole 4x4x16 slice. The times are simulated.
512 devices in a mesh: pm: 2 (over y_lo), ka: 128 (over x, z, core), isdf: 2 (over y_hi).
Axes of the slice: x: 4, y: 4 (y_hi: 2, y_lo: 2; y = y_hi * 2 + y_lo), z: 16, core: 2. Of those that a mesh axis runs over, the one named last changes fastest.
Arguments:
- amplitudes: bfloat16 [2, 2, 2, 256, 64, 256], P('pm', None, None, 'ka'), may hold values from -6 to 6
- conduction: bfloat16 [2, 256, 256, 512], P(None, 'ka', None, 'isdf'), may hold values from -0.375 to 0.375
- valence: bfloat16 [2, 256, 64, 512], P(None, 'ka'), may hold values from -0.75 to 0.75
- energy: float32 [256, 64, 256], P('ka', None, 'isdf'), may hold values from 0.5 to 2.5
- screened: bfloat16 [4, 2, 512, 512], P(None, None, 'isdf'), may hold values from -0.59765625 to 0.59765625
- coulomb: float32 [512, 512], P(None, 'isdf'), may hold values from -0.03125 to 0.03125
- mirror: int32 [256], P('ka'), may hold values from 0 to 255, as said below
- transfer_class: int32 [256, 256], P('ka'), may hold values from 0 to 3, as said below
Outputs:
- response: bfloat16 [2, 2, 2, 256, 64, 256], P('pm', None, None, 'ka', None, 'isdf')
Inputs may be any that keep to these rules, and one draw needn't show every extreme that they name: mirror[mirror[k]] = k; a k-point of block j (the aligned block of 2 k-points that holds it) has its mirror in block 127 - j. transfer_class[k, k2] depends only on (k - k2) mod 256.
All inputs are finite; a program needn't handle non-finite values.
Results may differ from a plain program's by a relative error of at most 0.015.
Values may be sent and summed in bfloat16 or wider, within the bound.
A program may use at most 128 MiB of HBM per device.

v0:
```python
import jax
import jax.numpy as jnp
from jax import lax
from jax.sharding import PartitionSpec as P

REACH = 2
HIGHEST = lax.Precision.HIGHEST


def swapped(block, axis, apart):
    count = lax.axis_size(axis)
    route = []
    for low in range(count):
        high = low | 1 << apart
        if high != low and high < count:
            route += [(low, high), (high, low)]
    return lax.ppermute(block, axis, route)


def shifted(value, axis, by):
    size = lax.axis_size(axis)
    return lax.ppermute(value, axis, [(i, (i + by) % size) for i in range(size)])


def pair_einsum(pattern, left, right, conjugate):

    def single(first, second):
        return jnp.einsum(pattern, first, second, preferred_element_type=jnp.float32)

    if conjugate:
        real_part = single(left[0], right[0]) + single(left[1], right[1])
        imag_part = single(left[1], right[0]) - single(left[0], right[1])
    else:
        real_part = single(left[0], right[0]) - single(left[1], right[1])
        imag_part = single(left[0], right[1]) + single(left[1], right[0])
    return (real_part, imag_part)


def conjugated(field):
    return jnp.stack([field[:, 0], -field[:, 1]], axis=1)


def coefficients(vector, conduction):
    real_part, imag_part = pair_einsum(
        "bkvc,kcm->bkvm", (vector[:, 0], vector[:, 1]), (conduction[0], conduction[1]), False
    )
    return jnp.stack([real_part, imag_part], axis=1).astype(jnp.bfloat16)


def amp_bits(field):
    for bit_number in range(lax.axis_size("ka").bit_length() - 1):
        field = swapped(field, "ka", bit_number)
    return field


def result_bits(field):
    for bit_number in range(lax.axis_size("ka").bit_length() - 1):
        field = swapped(field, "ka", bit_number)
    return field


def per_device(amplitudes, conduction, valence, energy, screened, coulomb, mirror, transfer_class):
    pm_index = lax.axis_index("pm")
    ka_index = lax.axis_index("ka")
    isdf_index = lax.axis_index("isdf")
    ka_count = lax.axis_size("ka")
    kpoint_count = conduction.shape[1]
    mu_count = conduction.shape[3]
    point_count = valence.shape[3]
    cond_share = energy.shape[2]
    vector_count = amplitudes.shape[1]
    is_plus = pm_index == 0
    parity = jnp.where(is_plus, 1.0, -1.0).astype(jnp.float32)
    exchange_weight = jnp.where(is_plus, 4.0, 0.0).astype(jnp.float32)
    local_amps = amplitudes[0]
    partner_amps = swapped(local_amps, "pm", 0)
    partner_side = jnp.where(is_plus, partner_amps, local_amps)
    distant_side = amp_bits(partner_side)
    direct = jnp.where(is_plus, local_amps, partner_amps).astype(jnp.float32)
    local_mirror = mirror - (ka_count - 1 - ka_index) * kpoint_count
    flipped = conjugated(jnp.take(distant_side, local_mirror, axis=2).astype(jnp.float32))
    vector = (direct + parity * flipped).astype(jnp.bfloat16)
    own_coef = coefficients(vector, conduction)
    valence_part = lax.dynamic_slice_in_dim(valence, isdf_index * mu_count, mu_count, 3)
    rho_real = jnp.einsum(
        "kvm,bkvm->bm", valence_part[0], own_coef[:, 0], preferred_element_type=jnp.float32
    )
    rho_real = rho_real + jnp.einsum(
        "kvm,bkvm->bm", valence_part[1], own_coef[:, 1], preferred_element_type=jnp.float32
    )
    rho_imag = jnp.einsum(
        "kvm,bkvm->bm", valence_part[0], own_coef[:, 1], preferred_element_type=jnp.float32
    )
    rho_imag = rho_imag - jnp.einsum(
        "kvm,bkvm->bm", valence_part[1], own_coef[:, 0], preferred_element_type=jnp.float32
    )
    density = jnp.stack([rho_real, rho_imag], axis=1)
    spread = jnp.einsum("nm,brm->brn", coulomb, density, precision=HIGHEST)
    spread = lax.psum(spread, ("ka", "isdf"))
    potential = lax.dynamic_slice_in_dim(spread, isdf_index * mu_count, mu_count, 2)
    class_ids = jnp.arange(screened.shape[0], dtype=jnp.int32)

    def accumulate(totals, coef_block, valence_block, source):
        pair_real, pair_imag = pair_einsum(
            "bqvm,qvn->bqmn",
            (coef_block[:, 0], coef_block[:, 1]),
            (valence_block[0], valence_block[1]),
            True,
        )
        pair_real = pair_real.astype(jnp.bfloat16)
        pair_imag = pair_imag.astype(jnp.bfloat16)
        classes = lax.dynamic_slice_in_dim(transfer_class, source * kpoint_count, kpoint_count, 1)
        selector = (classes[:, :, None] == class_ids).astype(jnp.bfloat16)
        total_real, total_imag = totals
        for visitor in range(kpoint_count):
            chosen = jnp.einsum(
                "kw,wrmn->rkmn", selector[:, visitor], screened, preferred_element_type=jnp.float32
            ).astype(jnp.bfloat16)
            screen_real = chosen[0][None].astype(jnp.float32)
            screen_imag = chosen[1][None].astype(jnp.float32)
            visit_real = pair_real[:, visitor][:, None].astype(jnp.float32)
            visit_imag = pair_imag[:, visitor][:, None].astype(jnp.float32)
            total_real = total_real + (screen_real * visit_real - screen_imag * visit_imag)
            total_imag = total_imag + (screen_real * visit_imag + screen_imag * visit_real)
        return (total_real, total_imag)

    payload = (vector, conduction, valence)

    def advance(moving, offset):
        return shifted((moving[0], moving[1], moving[2]), "ka", offset)

    def unpack(moving):
        return (coefficients(moving[0], moving[1]), moving[2])

    def visit(totals, moving, distance):
        coef_block, valence_block = unpack(moving)
        source = jnp.mod(ka_index + distance, ka_count)
        return accumulate(totals, coef_block, valence_block, source)

    zero_field = jnp.zeros((vector_count, kpoint_count, mu_count, point_count), jnp.float32)
    totals = accumulate((zero_field, zero_field), own_coef, valence, ka_index)
    below_item = payload
    for count_done in range(REACH):
        below_item = advance(below_item, 1)
        totals = visit(totals, below_item, -(count_done + 1))
    above_item = payload
    for count_done in range(REACH):
        above_item = advance(above_item, -1)
        totals = visit(totals, above_item, count_done + 1)
    sum_real = totals[0].astype(jnp.bfloat16)
    sum_imag = totals[1].astype(jnp.bfloat16)
    back_real, back_imag = pair_einsum(
        "bkmn,kvn->bkvm", (sum_real, sum_imag), (valence[0], valence[1]), False
    )
    potential_real = potential[:, 0][:, None, None, :]
    potential_imag = potential[:, 1][:, None, None, :]
    exchange_real = potential_real * valence_part[0] - potential_imag * valence_part[1]
    exchange_imag = potential_real * valence_part[1] + potential_imag * valence_part[0]
    field_real = (exchange_weight * exchange_real - back_real).astype(jnp.bfloat16)
    field_imag = (exchange_weight * exchange_imag - back_imag).astype(jnp.bfloat16)
    out_real, out_imag = pair_einsum(
        "bkvm,kcm->bkvc", (field_real, field_imag), (conduction[0], conduction[1]), True
    )
    partial_out = jnp.stack([out_real, out_imag], axis=1)
    summed = lax.psum_scatter(
        partial_out.astype(jnp.bfloat16), "isdf", scatter_dimension=4, tiled=True
    ).astype(jnp.float32)
    vector_part = lax.dynamic_slice_in_dim(vector, isdf_index * cond_share, cond_share, 4).astype(
        jnp.float32
    )
    channel_out = (energy[None, None] * vector_part + summed).astype(jnp.bfloat16)
    partner_out = swapped(channel_out, "pm", 0)
    blended = (
        0.5 * (partner_out.astype(jnp.float32) + parity * channel_out.astype(jnp.float32))
    ).astype(jnp.bfloat16)
    distant_out = result_bits(blended)
    reflected = conjugated(jnp.take(distant_out, local_mirror, axis=2))
    result = jnp.where(is_plus, blended, reflected)
    return result[None]


def solution(mesh):
    return jax.shard_map(
        per_device,
        mesh=mesh,
        in_specs=(
            P("pm", None, None, "ka", None, None),
            P(None, "ka", None, "isdf"),
            P(None, "ka", None, None),
            P("ka", None, "isdf"),
            P(None, None, "isdf", None),
            P(None, "isdf"),
            P("ka"),
            P("ka", None),
        ),
        out_specs=P("pm", None, None, "ka", None, "isdf"),
        check_vma=False,
    )
```

profile of v0, /device:TPU:2, one launch (start us, length us, event | category | flops | bytes accessed | tf_op | source)
XLA Modules:
  0.0 1090.2 jit_solution(7875653439164302398)
XLA Ops:
  6.5 2.0 collective-permute-start.9
  8.6 10.8 collective-permute-start.15
  21.3 5.8 collective-permute-start.16
  28.1 3.5 collective-permute-start
  32.8 3.2 copy.91
  36.0 2.2 fusion.12
  38.2 2.2 fusion.13
  40.6 2.2 fusion.14
  42.8 2.2 fusion.15
  45.2 2.2 fusion.16
  47.4 2.2 fusion.17
  49.8 2.2 fusion.18
  52.0 2.4 fusion.19
  54.6 2.2 fusion.10
  56.8 2.2 fusion.11
  59.0 3.0 fusion.79
  62.0 2.0 fusion.75
  64.1 2.1 fusion.71
  66.2 2.1 fusion.67
  68.3 2.1 collective-permute-start.1
  70.4 2.1 fusion.63
  72.5 2.0 collective-permute-start.2
  74.6 2.1 fusion.59
  76.7 6.6 collective-permute-done.2
  85.2 2.0 fusion.55
  87.2 12.3 %collective-permute-done.3 = bf16[2,2,2,64,256]{4,3,0,2,1:T(8,128)(2,1)S(1)} collective-permute-done((bf16[2,2,2,64,256]{4,3,0,2,1:T(8,128)(2,1)S(1)}, bf16[2,2,2,64,256]{4,3,0,2,1:T(8,128)(2,1)S(1)}, u32[]{:S(2)}, u32[]{:S(2)}) %collective-permute-start.3) | collective-permute-done | bytes 262176 | tf_op jit(solution)/shard_map/ppermute | solution.py:17
  99.5 2.4 collective-permute-start.4
  101.9 2.0 fusion.51
  104.0 22.7 %collective-permute-done.4 = bf16[2,2,2,64,256]{4,3,0,2,1:T(8,128)(2,1)S(1)} collective-permute-done((bf16[2,2,2,64,256]{4,3,0,2,1:T(8,128)(2,1)S(1)}, bf16[2,2,2,64,256]{4,3,0,2,1:T(8,128)(2,1)S(1)}, u32[]{:S(2)}, u32[]{:S(2)}) %collective-permute-start.4) | collective-permute-done | bytes 262176 | tf_op jit(solution)/shard_map/ppermute | solution.py:17
  126.6 14.7 %collective-permute-start.5 = (bf16[2,2,2,64,256]{4,3,0,2,1:T(8,128)(2,1)S(1)}, bf16[2,2,2,64,256]{4,3,0,2,1:T(8,128)(2,1)S(1)}, u32[]{:S(2)}, u32[]{:S(2)}) collective-permute-start(bf16[2,2,2,64,256]{4,3,0,2,1:T(8,128)(2,1)S(1)} %collective-permute-done.4), channel_id=1, source_target_pairs={{0,32},{32,0},{2,34},{34,2},{4,36},{36,4},{6,38},{38,6},{8,40},{40... | collective-permute-start | bytes 786440 | tf_op jit(solution)/shard_map/ppermute | solution.py:17
  141.3 2.1 fusion.87
  143.4 14.8 %collective-permute-done.5 = bf16[2,2,2,64,256]{4,3,0,2,1:T(8,128)(2,1)S(1)} collective-permute-done((bf16[2,2,2,64,256]{4,3,0,2,1:T(8,128)(2,1)S(1)}, bf16[2,2,2,64,256]{4,3,0,2,1:T(8,128)(2,1)S(1)}, u32[]{:S(2)}, u32[]{:S(2)}) %collective-permute-start.5) | collective-permute-done | bytes 262176 | tf_op jit(solution)/shard_map/ppermute | solution.py:17
  158.2 2.7 collective-permute-start.6
  161.0 2.1 fusion.83
  163.1 5.4 collective-permute-done.6
  168.4 4.2 collective-permute-start.7
  196.8 2.0 collective-permute-start.13
  198.8 5.8 collective-permute-start.19
  206.5 5.8 collective-permute-start.18
  214.0 2.2 gather_fusion
  228.5 583.0 %psum.7 = f32[2,2,512]{2,1,0:T(2,128)S(1)} all-reduce(f32[2,2,512]{2,1,0:T(2,128)S(1)} %fusion.90), channel_id=1, replica_groups=mesh['pm'=2,'ka'=128,'isdf'=2] {'ka','isdf'}, use_global_device_ids=true, to_apply=%region_0.1 | all-reduce | flops 2048 | bytes 16384 | tf_op jit(solution)/shard_map/psum | solution.py:99
  828.4 2.2 fusion.76
  830.6 2.7 collective-permute-start.11
  843.4 2.2 fusion.60
  845.6 5.3 collective-permute-start.17
  861.0 2.2 fusion.68
  874.3 2.3 fusion.52
  878.6 9.2 add_convert_fusion
  887.9 9.5 add_convert_fusion.1
  901.8 92.5 %reduce-scatter.4.cloned.1.call-done = bf16[128,512]{1,0:T(8,128)(2,1)} async-done(((bf16[256,512]{1,0:T(8,128)(2,1)}), bf16[128,512]{1,0:T(8,128)(2,1)}) %reduce-scatter.4.cloned.1.call-update) | async-done | bytes 131088
  996.5 2.5 collective-permute-start.20
  999.0 4.7 collective-permute-done.20
  1007.0 3.5 collective-permute-start.22
  1010.4 4.0 collective-permute-done.22
  1014.4 4.4 collective-permute-start.23
  1018.9 5.9 collective-permute-done.23
  1024.7 7.6 collective-permute-start.24
  1032.4 9.9 collective-permute-done.24
  1042.2 12.0 %collective-permute-start.25 = (bf16[2,2,2,64,128]{4,3,0,2,1:T(8,128)(2,1)S(1)}, bf16[2,2,2,64,128]{4,3,0,2,1:T(8,128)(2,1)S(1)}, u32[]{:S(2)}, u32[]{:S(2)}) collective-permute-start(bf16[2,2,2,64,128]{4,3,0,2,1:T(8,128)(2,1)S(1)} %collective-permute-done.24), channel_id=1, source_target_pairs={{0,32},{32,0},{2,34},{34,2},{4,36},{36,4},{6,38},{38,6},{8,40},{40... | collective-permute-start | bytes 393224 | tf_op jit(solution)/shard_map/ppermute | solution.py:17
  1054.2 12.1 %collective-permute-done.25 = bf16[2,2,2,64,128]{4,3,0,2,1:T(8,128)(2,1)S(1)} collective-permute-done((bf16[2,2,2,64,128]{4,3,0,2,1:T(8,128)(2,1)S(1)}, bf16[2,2,2,64,128]{4,3,0,2,1:T(8,128)(2,1)S(1)}, u32[]{:S(2)}, u32[]{:S(2)}) %collective-permute-start.25) | collective-permute-done | bytes 131104 | tf_op jit(solution)/shard_map/ppermute | solution.py:17
  1066.3 2.5 collective-permute-start.26
  1068.8 4.4 collective-permute-done.26
  1073.2 3.9 collective-permute-start.27
  1077.1 4.4 collective-permute-done.27
  (253 shorter events, 107.3 us)
Async XLA Ops:
  6.5 221.4 %copy-start = (f32[512,256]{1,0:T(8,128)S(1)}, f32[512,256]{1,0:T(8,128)}, u32[]{:S(2)}) copy-start(f32[512,256]{1,0:T(8,128)} %param.13) | copy-start | bytes 1572868
  6.5 987.7 %reduce-scatter.4.cloned.1.call-start = ((), (), s32[]{:S(2)}) async-start(), calls=%async_computation.1 | async-start | bytes 393216
  6.5 198.1 %collective-permute-start.9 = (bf16[2,2,256,256]{3,2,1,0:T(8,128)(2,1)}, bf16[2,2,256,256]{3,2,1,0:T(8,128)(2,1)}, u32[]{:S(2)}, u32[]{:S(2)}) collective-permute-start(bf16[2,2,256,256]{3,2,1,0:T(8,128)(2,1)} %param.9), channel_id=1, source_target_pairs={{0,2},{2,4},{4,6},{6,8},{8,10},{10,12},{12,14},{14,16},{16,18},{18... | collective-permute-start | bytes 1572872 | tf_op jit(solution)/shard_map/ppermute | solution.py:22
  8.6 197.9 %collective-permute-start.15 = (bf16[2,2,256,256]{3,2,1,0:T(8,128)(2,1)}, bf16[2,2,256,256]{3,2,1,0:T(8,128)(2,1)}, u32[]{:S(2)}, u32[]{:S(2)}) collective-permute-start(bf16[2,2,256,256]{3,2,1,0:T(8,128)(2,1)} %param.9), channel_id=1, source_target_pairs={{0,254},{2,0},{4,2},{6,4},{8,6},{10,8},{12,10},{14,12},{16,14},{18... | collective-permute-start | bytes 1572872 | tf_op jit(solution)/shard_map/ppermute | solution.py:22
  19.4 177.4 %collective-permute-start.10 = (bf16[2,2,64,512]{3,2,1,0:T(8,128)(2,1)}, bf16[2,2,64,512]{3,2,1,0:T(8,128)(2,1)}, u32[]{:S(2)}, u32[]{:S(2)}) collective-permute-start(bf16[2,2,64,512]{3,2,1,0:T(8,128)(2,1)} %param.10), channel_id=1, source_target_pairs={{0,2},{2,4},{4,6},{6,8},{8,10},{10,12},{12,14},{14,16},{16,18},{18... | collective-permute-start | bytes 786440 | tf_op jit(solution)/shard_map/ppermute | solution.py:22
  21.3 177.5 %collective-permute-start.16 = (bf16[2,2,64,512]{3,2,1,0:T(8,128)(2,1)}, bf16[2,2,64,512]{3,2,1,0:T(8,128)(2,1)}, u32[]{:S(2)}, u32[]{:S(2)}) collective-permute-start(bf16[2,2,64,512]{3,2,1,0:T(8,128)(2,1)} %param.10), channel_id=1, source_target_pairs={{0,254},{2,0},{4,2},{6,4},{8,6},{10,8},{12,10},{14,12},{16,14},{18... | collective-permute-start | bytes 786440 | tf_op jit(solution)/shard_map/ppermute | solution.py:22
  28.1 40.2 %collective-permute-start = (bf16[2,2,2,64,256]{4,3,0,2,1:T(8,128)(2,1)S(1)}, bf16[2,2,2,64,256]{4,3,0,2,1:T(8,128)(2,1)S(1)}, u32[]{:S(2)}, u32[]{:S(2)}) collective-permute-start(bf16[2,2,2,64,256]{4,3,0,2,1:T(8,128)(2,1)S(1)} %bitcast.651), channel_id=1, source_target_pairs={{0,256},{256,0},{1,257},{257,1},{2,258},{258,2},{3,259},{259,3},{4... | collective-permute-start | bytes 786440 | tf_op jit(solution)/shard_map/ppermute | solution.py:17
  59.0 3.0 copy-start.53
  66.2 4.2 copy-start.51
  68.3 6.3 copy-start.50
  68.3 8.4 copy-start.55
  68.3 4.2 collective-permute-start.1
  72.5 12.6 %copy-start.49 = (bf16[2,2,256,512]{3,1,2,0:T(2,128)(2,1)S(1)}, bf16[2,2,256,512]{3,1,2,0:T(2,128)(2,1)}, u32[]{:S(2)}) copy-start(bf16[2,2,256,512]{3,1,2,0:T(2,128)(2,1)} %fusion.18) | copy-start | bytes 3145732
  72.5 10.7 collective-permute-start.2
  76.7 25.3 %copy-start.48 = (bf16[2,2,256,512]{3,1,2,0:T(2,128)(2,1)S(1)}, bf16[2,2,256,512]{3,1,2,0:T(2,128)(2,1)}, u32[]{:S(2)}) copy-start(bf16[2,2,256,512]{3,1,2,0:T(2,128)(2,1)} %fusion.19) | copy-start | bytes 3145732
  83.2 16.3 %collective-permute-start.3 = (bf16[2,2,2,64,256]{4,3,0,2,1:T(8,128)(2,1)S(1)}, bf16[2,2,2,64,256]{4,3,0,2,1:T(8,128)(2,1)S(1)}, u32[]{:S(2)}, u32[]{:S(2)}) collective-permute-start(bf16[2,2,2,64,256]{4,3,0,2,1:T(8,128)(2,1)S(1)} %collective-permute-done.2), channel_id=1, source_target_pairs={{0,8},{8,0},{2,10},{10,2},{4,12},{12,4},{6,14},{14,6},{16,24},{24,... | collective-permute-start | bytes 786440 | tf_op jit(solution)/shard_map/ppermute | solution.py:17
  87.2 54.1 %copy-start.47 = (bf16[2,2,256,512]{3,1,2,0:T(2,128)(2,1)S(1)}, bf16[2,2,256,512]{3,1,2,0:T(2,128)(2,1)}, u32[]{:S(2)}) copy-start(bf16[2,2,256,512]{3,1,2,0:T(2,128)(2,1)} %fusion.10) | copy-start | bytes 3145732
  99.5 27.1 %collective-permute-start.4 = (bf16[2,2,2,64,256]{4,3,0,2,1:T(8,128)(2,1)S(1)}, bf16[2,2,2,64,256]{4,3,0,2,1:T(8,128)(2,1)S(1)}, u32[]{:S(2)}, u32[]{:S(2)}) collective-permute-start(bf16[2,2,2,64,256]{4,3,0,2,1:T(8,128)(2,1)S(1)} %collective-permute-done.3), channel_id=1, source_target_pairs={{0,16},{16,0},{2,18},{18,2},{4,20},{20,4},{6,22},{22,6},{8,24},{24... | collective-permute-start | bytes 786440 | tf_op jit(solution)/shard_map/ppermute | solution.py:17
  103.9 57.0 %copy-start.46 = (bf16[2,2,256,512]{3,1,2,0:T(2,128)(2,1)S(1)}, bf16[2,2,256,512]{3,1,2,0:T(2,128)(2,1)}, u32[]{:S(2)}) copy-start(bf16[2,2,256,512]{3,1,2,0:T(2,128)(2,1)} %fusion.11) | copy-start | bytes 3145732
  126.6 31.6 %collective-permute-start.5 = (bf16[2,2,2,64,256]{4,3,0,2,1:T(8,128)(2,1)S(1)}, bf16[2,2,2,64,256]{4,3,0,2,1:T(8,128)(2,1)S(1)}, u32[]{:S(2)}, u32[]{:S(2)}) collective-permute-start(bf16[2,2,2,64,256]{4,3,0,2,1:T(8,128)(2,1)S(1)} %collective-permute-done.4), channel_id=1, source_target_pairs={{0,32},{32,0},{2,34},{34,2},{4,36},{36,4},{6,38},{38,6},{8,40},{40... | collective-permute-start | bytes 786440 | tf_op jit(solution)/shard_map/ppermute | solution.py:17
  143.4 29.3 %copy-start.59 = (s32[2]{0:T(128)S(1)}, s32[2]{0:T(128)}, u32[]{:S(2)}) copy-start(s32[2]{0:T(128)} %param.14) | copy-start | bytes 28
  158.2 10.2 collective-permute-start.6
  168.4 43.9 %collective-permute-start.7 = (bf16[2,2,2,64,256]{4,3,0,2,1:T(8,128)(2,1)}, bf16[2,2,2,64,256]{4,3,0,2,1:T(8,128)(2,1)}, u32[]{:S(2)}, u32[]{:S(2)}) collective-permute-start(bf16[2,2,2,64,256]{4,3,0,2,1:T(8,128)(2,1)} %collective-permute-done.6), channel_id=1, source_target_pairs={{0,128},{128,0},{2,130},{130,2},{4,132},{132,4},{6,134},{134,6},{8... | collective-permute-start | bytes 786440 | tf_op jit(solution)/shard_map/ppermute | solution.py:17
  172.9 2.7 copy-start.29
  196.8 22.3 %copy-start.21 = (bf16[2,2,256,256]{3,2,1,0:T(8,128)(2,1)S(1)}, bf16[2,2,256,256]{3,2,1,0:T(8,128)(2,1)}, u32[]{:S(2)}) copy-start(bf16[2,2,256,256]{3,2,1,0:T(8,128)(2,1)} %param.9) | copy-start | bytes 1572868
  196.8 658.7 %collective-permute-start.13 = (bf16[2,2,64,512]{3,2,1,0:T(8,128)(2,1)}, bf16[2,2,64,512]{3,2,1,0:T(8,128)(2,1)}, u32[]{:S(2)}, u32[]{:S(2)}) collective-permute-start(bf16[2,2,64,512]{3,2,1,0:T(8,128)(2,1)} %collective-permute-done.10), channel_id=1, source_target_pairs={{0,2},{2,4},{4,6},{6,8},{8,10},{10,12},{12,14},{14,16},{16,18},{18... | collective-permute-start | bytes 786440 | tf_op jit(solution)/shard_map/ppermute | solution.py:22
  198.8 669.1 %collective-permute-start.19 = (bf16[2,2,64,512]{3,2,1,0:T(8,128)(2,1)}, bf16[2,2,64,512]{3,2,1,0:T(8,128)(2,1)}, u32[]{:S(2)}, u32[]{:S(2)}) collective-permute-start(bf16[2,2,64,512]{3,2,1,0:T(8,128)(2,1)} %collective-permute-done.16), channel_id=1, source_target_pairs={{0,254},{2,0},{4,2},{6,4},{8,6},{10,8},{12,10},{14,12},{16,14},{18... | collective-permute-start | bytes 786440 | tf_op jit(solution)/shard_map/ppermute | solution.py:22
  204.6 641.0 %collective-permute-start.12 = (bf16[2,2,256,256]{3,2,1,0:T(8,128)(2,1)}, bf16[2,2,256,256]{3,2,1,0:T(8,128)(2,1)}, u32[]{:S(2)}, u32[]{:S(2)}) collective-permute-start(bf16[2,2,256,256]{3,2,1,0:T(8,128)(2,1)} %collective-permute-done.9), channel_id=1, source_target_pairs={{0,2},{2,4},{4,6},{6,8},{8,10},{10,12},{12,14},{14,16},{16,18},{18... | collective-permute-start | bytes 1572872 | tf_op jit(solution)/shard_map/ppermute | solution.py:22
  206.5 656.7 %collective-permute-start.18 = (bf16[2,2,256,256]{3,2,1,0:T(8,128)(2,1)}, bf16[2,2,256,256]{3,2,1,0:T(8,128)(2,1)}, u32[]{:S(2)}, u32[]{:S(2)}) collective-permute-start(bf16[2,2,256,256]{3,2,1,0:T(8,128)(2,1)} %collective-permute-done.15), channel_id=1, source_target_pairs={{0,254},{2,0},{4,2},{6,4},{8,6},{10,8},{12,10},{14,12},{16,14},{18... | collective-permute-start | bytes 1572872 | tf_op jit(solution)/shard_map/ppermute | solution.py:22
  219.1 7.1 copy-start.56
  219.1 7.1 copy-start.57
  221.3 594.7 %collective-permute-start.8 = (bf16[2,2,2,64,256]{4,3,0,2,1:T(8,128)(2,1)}, bf16[2,2,2,64,256]{4,3,0,2,1:T(8,128)(2,1)}, u32[]{:S(2)}, u32[]{:S(2)}) collective-permute-start(bf16[2,2,2,64,256]{4,3,0,2,1:T(8,128)(2,1)} %fusion.89), channel_id=1, source_target_pairs={{0,2},{2,4},{4,6},{6,8},{8,10},{10,12},{12,14},{14,16},{16,18},{18... | collective-permute-start | bytes 786440 | tf_op jit(solution)/shard_map/ppermute | solution.py:22
  228.5 584.7 %copy-start.45 = (bf16[2,2,64,256]{3,2,1,0:T(8,128)(2,1)S(1)}, bf16[2,2,64,256]{3,2,1,0:T(8,128)(2,1)}, u32[]{:S(2)}) copy-start(bf16[2,2,64,256]{3,2,1,0:T(8,128)(2,1)} %get-tuple-element.66) | copy-start | bytes 393220
  816.0 60.6 %copy-start.20 = (f32[2,256,512]{2,1,0:T(8,128)}, f32[2,256,512]{2,1,0:T(8,128)S(1)}, u32[]{:S(2)}) copy-start(f32[2,256,512]{2,1,0:T(8,128)S(1)} %get-tuple-element.15) | copy-start | bytes 3145732
  816.0 14.6 %collective-permute-start.14 = (bf16[2,2,2,64,256]{4,3,0,2,1:T(8,128)(2,1)}, bf16[2,2,2,64,256]{4,3,0,2,1:T(8,128)(2,1)S(1)}, u32[]{:S(2)}, u32[]{:S(2)}) collective-permute-start(bf16[2,2,2,64,256]{4,3,0,2,1:T(8,128)(2,1)} %fusion.89), channel_id=1, source_target_pairs={{0,254},{2,0},{4,2},{6,4},{8,6},{10,8},{12,10},{14,12},{16,14},{18... | collective-permute-start | bytes 786440 | tf_op jit(solution)/shard_map/ppermute | solution.py:22
  830.6 20.3 %collective-permute-start.11 = (bf16[2,2,2,64,256]{4,3,0,2,1:T(8,128)(2,1)}, bf16[2,2,2,64,256]{4,3,0,2,1:T(8,128)(2,1)S(1)}, u32[]{:S(2)}, u32[]{:S(2)}) collective-permute-start(bf16[2,2,2,64,256]{4,3,0,2,1:T(8,128)(2,1)} %collective-permute-done.8), channel_id=1, source_target_pairs={{0,2},{2,4},{4,6},{6,8},{8,10},{10,12},{12,14},{14,16},{16,18},{18... | collective-permute-start | bytes 786440 | tf_op jit(solution)/shard_map/ppermute | solution.py:22
  845.6 17.6 %collective-permute-start.17 = (bf16[2,2,2,64,256]{4,3,0,2,1:T(8,128)(2,1)S(1)}, bf16[2,2,2,64,256]{4,3,0,2,1:T(8,128)(2,1)S(1)}, u32[]{:S(2)}, u32[]{:S(2)}) collective-permute-start(bf16[2,2,2,64,256]{4,3,0,2,1:T(8,128)(2,1)S(1)} %collective-permute-done.14), channel_id=1, source_target_pairs={{0,254},{2,0},{4,2},{6,4},{8,6},{10,8},{12,10},{14,12},{16,14},{18... | collective-permute-start | bytes 786440 | tf_op jit(solution)/shard_map/ppermute | solution.py:22
  865.5 11.0 %copy-start.19 = (f32[2,256,512]{2,1,0:T(8,128)S(1)}, f32[2,256,512]{2,1,0:T(8,128)}, u32[]{:S(2)}) copy-start(f32[2,256,512]{2,1,0:T(8,128)} %copy.99) | copy-start | bytes 3145732
  867.9 8.6 copy-start.16
  868.0 8.6 copy-start.17
  868.0 8.6 copy-start.18
  869.5 7.1 copy-start.14
  869.5 7.1 copy-start.15
  871.1 5.5 copy-start.11
  871.1 5.5 copy-start.12
  871.1 5.5 copy-start.13
  872.6 4.0 copy-start.8
  872.7 4.0 copy-start.9
  872.7 4.0 copy-start.10
  874.2 2.7 copy-start.3
  874.2 3.5 copy-start.4
  874.3 3.7 copy-start.5
  874.3 4.0 copy-start.6
  874.3 4.3 copy-start.7
  900.0 95.6 %copy-start.58 = (f32[2,64,128]{2,1,0:T(8,128)S(1)}, f32[2,64,128]{2,1,0:T(8,128)}, u32[]{:S(2)}) copy-start(f32[2,64,128]{2,1,0:T(8,128)} %param.11) | copy-start | bytes 196612
  900.7 182.2 %copy-start.1 = (f32[512,256]{1,0:T(8,128)S(1)}, f32[512,256]{1,0:T(8,128)}, u32[]{:S(2)}) copy-start(f32[512,256]{1,0:T(8,128)} %param.13) | copy-start | bytes 1572868
  996.5 7.1 collective-permute-start.20
  1003.7 3.2 collective-permute-start.21
  1007.0 7.4 collective-permute-start.22
  1014.4 10.3 collective-permute-start.23
  1024.7 17.5 %collective-permute-start.24 = (bf16[2,2,2,64,128]{4,3,0,2,1:T(8,128)(2,1)S(1)}, bf16[2,2,2,64,128]{4,3,0,2,1:T(8,128)(2,1)S(1)}, u32[]{:S(2)}, u32[]{:S(2)}) collective-permute-start(bf16[2,2,2,64,128]{4,3,0,2,1:T(8,128)(2,1)S(1)} %collective-permute-done.23), channel_id=1, source_target_pairs={{0,16},{16,0},{2,18},{18,2},{4,20},{20,4},{6,22},{22,6},{8,24},{24... | collective-permute-start | bytes 393224 | tf_op jit(solution)/shard_map/ppermute | solution.py:17
  1042.2 24.1 %collective-permute-start.25 = (bf16[2,2,2,64,128]{4,3,0,2,1:T(8,128)(2,1)S(1)}, bf16[2,2,2,64,128]{4,3,0,2,1:T(8,128)(2,1)S(1)}, u32[]{:S(2)}, u32[]{:S(2)}) collective-permute-start(bf16[2,2,2,64,128]{4,3,0,2,1:T(8,128)(2,1)S(1)} %collective-permute-done.24), channel_id=1, source_target_pairs={{0,32},{32,0},{2,34},{34,2},{4,36},{36,4},{6,38},{38,6},{8,40},{40... | collective-permute-start | bytes 393224 | tf_op jit(solution)/shard_map/ppermute | solution.py:17
  1066.3 6.8 collective-permute-start.26
  1073.2 8.4 collective-permute-start.27
  (25 other events, 54.5 us)
Sparse Core Ops, SparseCore 0:
  901.9 92.3 reduce-scatter.3
where the time goes:
time: 1100 us; the launch traced here: 1090 us
  blocking collectives  583 us (53%)
  waiting for transfers between devices  201 us (18%)
  starting transfers between devices  120 us (11%)
  matrix products  76.2 us (7%)
  other arithmetic  56.5 us (5%)
  local copies, waits for them, and re-layouts  38.9 us (4%)
  between operations  15.1 us (1%)
    psum x1, blocking collectives, per_device(): spread = lax.psum(spread, ('ka', 'isdf'))  583 us
    ppermute x16, waiting for transfers between devices, swapped(): return lax.ppermute(block, axis, route)  108 us
    unnamed x2, waiting for transfers between devices  92.5 us
    ppermute x16, starting transfers between devices, swapped(): return lax.ppermute(block, axis, route)  71.8 us
    dot_general x48, matrix products, single(): jnp.einsum(pattern, first, second, preferred_element_type=jnp.float32)  53.3 us
    ppermute x12, starting transfers between devices, shifted(): lax.ppermute(value, axis, [(i, (i + by) % size) for i in range(size)])  47.7 us
    dot_general x10, matrix products, accumulate(): jnp.einsum('kw,wrmn->rkmn', selector[:, visitor], screened, preferred_ele...  22.4 us
  transfers between devices with their start and end apart: 29, of which 14 were waited for; matrix products, arithmetic and copies ran while one was open for 12% of the time, Pallas kernels for 0%

commit v1 on v0

--- a/solution.py
+++ b/solution.py
@@ -96,7 +96,7 @@
     )
     density = jnp.stack([rho_real, rho_imag], axis=1)
     spread = jnp.einsum("nm,brm->brn", coulomb, density, precision=HIGHEST)
-    spread = lax.psum(spread, ("ka", "isdf"))
+    spread = lax.psum(lax.psum(spread, "isdf"), "ka")
     potential = lax.dynamic_slice_in_dim(spread, isdf_index * mu_count, mu_count, 2)
     class_ids = jnp.arange(screened.shape[0], dtype=jnp.int32)
 

time: 1100 us -> 703 us (0.64)
  blocking collectives: 583 us -> 221 us
  waiting for transfers between devices: 201 us -> 165 us
    psum x1 -> x2, blocking collectives: 583 us -> 221 us  [per_device(): spread = lax.psum(lax.psum(spread, 'isdf'), 'ka')]
    unnamed x2, waiting for transfers between devices: 92.5 us -> 56.5 us
  transfers between devices with their start and end apart: 29 -> 29, of which waited for: 14 -> 14; matrix products, arithmetic and copies ran while one was open for 12% -> 19% of each run, Pallas kernels for 0% -> 0%
where the time goes in v1:
time: 703 us; the launch traced here: 693 us
  blocking collectives  221 us (31%)
  waiting for transfers between devices  165 us (23%)
  starting transfers between devices  120 us (17%)
  matrix products  76.2 us (11%)
  other arithmetic  56.4 us (8%)
  local copies, waits for them, and re-layouts  38.9 us (6%)
  between operations  15.1 us (2%)
    psum x2, blocking collectives, per_device(): spread = lax.psum(lax.psum(spread, 'isdf'), 'ka')  221 us
    ppermute x16, waiting for transfers between devices, swapped(): return lax.ppermute(block, axis, route)  108 us
    ppermute x16, starting transfers between devices, swapped(): return lax.ppermute(block, axis, route)  71.8 us
    unnamed x2, waiting for transfers between devices  56.5 us
    dot_general x48, matrix products, single(): jnp.einsum(pattern, first, second, preferred_element_type=jnp.float32)  53.3 us
    ppermute x12, starting transfers between devices, shifted(): lax.ppermute(value, axis, [(i, (i + by) % size) for i in range(size)])  47.7 us
    dot_general x10, matrix products, accumulate(): jnp.einsum('kw,wrmn->rkmn', selector[:, visitor], screened, preferred_ele...  22.3 us
    mul x10, other arithmetic, accumulate(): screen_real * visit_real - screen_imag * visit_imag  21.6 us
  transfers between devices with their start and end apart: 29, of which 14 were waited for; matrix products, arithmetic and copies ran while one was open for 19% of the time, Pallas kernels for 0%

profile of v1, /device:TPU:2, one launch (start us, length us, event | category | flops | bytes accessed | tf_op | source)
XLA Modules:
  0.0 692.6 jit_solution(1709878176859799108)
XLA Ops:
  6.5 2.0 collective-permute-start.9
  8.6 10.8 %collective-permute-start.15 = (bf16[2,2,256,256]{3,2,1,0:T(8,128)(2,1)}, bf16[2,2,256,256]{3,2,1,0:T(8,128)(2,1)}, u32[]{:S(2)}, u32[]{:S(2)}) collective-permute-start(bf16[2,2,256,256]{3,2,1,0:T(8,128)(2,1)} %param.9), channel_id=1, source_target_pairs={{0,254},{2,0},{4,2},{6,4},{8,6},{10,8},{12,10},{14,12},{16,14},{18... | collective-permute-start | bytes 1572872 | tf_op jit(solution)/shard_map/ppermute | solution.py:22
  21.3 5.8 collective-permute-start.16
  28.1 3.5 collective-permute-start
  32.8 3.2 copy.91
  36.0 2.2 fusion.12
  38.2 2.2 fusion.13
  40.6 2.2 fusion.14
  42.8 2.2 fusion.15
  45.2 2.2 fusion.16
  47.4 2.2 fusion.17
  49.8 2.2 fusion.18
  52.0 2.4 fusion.19
  54.6 2.2 fusion.10
  56.8 2.2 fusion.11
  59.0 3.0 fusion.79
  62.0 2.1 fusion.75
  64.0 2.1 fusion.71
  66.1 2.1 fusion.67
  68.3 2.1 collective-permute-start.1
  70.4 2.1 fusion.63
  72.5 2.0 collective-permute-start.2
  74.5 2.1 fusion.59
  76.6 6.6 collective-permute-done.2
  87.2 12.3 %collective-permute-done.3 = bf16[2,2,2,64,256]{4,3,0,2,1:T(8,128)(2,1)S(1)} collective-permute-done((bf16[2,2,2,64,256]{4,3,0,2,1:T(8,128)(2,1)S(1)}, bf16[2,2,2,64,256]{4,3,0,2,1:T(8,128)(2,1)S(1)}, u32[]{:S(2)}, u32[]{:S(2)}) %collective-permute-start.3) | collective-permute-done | bytes 262176 | tf_op jit(solution)/shard_map/ppermute | solution.py:17
  99.5 2.4 collective-permute-start.4
  101.9 2.0 fusion.51
  103.9 22.7 %collective-permute-done.4 = bf16[2,2,2,64,256]{4,3,0,2,1:T(8,128)(2,1)S(1)} collective-permute-done((bf16[2,2,2,64,256]{4,3,0,2,1:T(8,128)(2,1)S(1)}, bf16[2,2,2,64,256]{4,3,0,2,1:T(8,128)(2,1)S(1)}, u32[]{:S(2)}, u32[]{:S(2)}) %collective-permute-start.4) | collective-permute-done | bytes 262176 | tf_op jit(solution)/shard_map/ppermute | solution.py:17
  126.6 14.7 %collective-permute-start.5 = (bf16[2,2,2,64,256]{4,3,0,2,1:T(8,128)(2,1)S(1)}, bf16[2,2,2,64,256]{4,3,0,2,1:T(8,128)(2,1)S(1)}, u32[]{:S(2)}, u32[]{:S(2)}) collective-permute-start(bf16[2,2,2,64,256]{4,3,0,2,1:T(8,128)(2,1)S(1)} %collective-permute-done.4), channel_id=1, source_target_pairs={{0,32},{32,0},{2,34},{34,2},{4,36},{36,4},{6,38},{38,6},{8,40},{40... | collective-permute-start | bytes 786440 | tf_op jit(solution)/shard_map/ppermute | solution.py:17
  141.3 2.1 fusion.87
  143.3 14.9 %collective-permute-done.5 = bf16[2,2,2,64,256]{4,3,0,2,1:T(8,128)(2,1)S(1)} collective-permute-done((bf16[2,2,2,64,256]{4,3,0,2,1:T(8,128)(2,1)S(1)}, bf16[2,2,2,64,256]{4,3,0,2,1:T(8,128)(2,1)S(1)}, u32[]{:S(2)}, u32[]{:S(2)}) %collective-permute-start.5) | collective-permute-done | bytes 262176 | tf_op jit(solution)/shard_map/ppermute | solution.py:17
  158.2 2.7 collective-permute-start.6
  160.9 2.1 fusion.83
  163.0 5.4 collective-permute-done.6
  168.4 4.2 collective-permute-start.7
  196.7 2.0 collective-permute-start.13
  198.8 5.8 collective-permute-start.19
  206.5 5.8 collective-permute-start.18
  213.9 2.2 gather_fusion
  228.4 6.6 psum.14
  235.1 214.8 %psum.15 = f32[2,2,512]{2,1,0:T(2,128)S(1)} all-reduce(f32[2,2,512]{2,1,0:T(2,128)S(1)} %psum.14), channel_id=1, replica_groups=mesh['pm'=2,'ka'=128,'isdf'=2] {'ka'}, use_global_device_ids=true, to_apply=%region_1.2 | all-reduce | flops 2048 | bytes 16384 | tf_op jit(solution)/shard_map/psum | solution.py:99
  466.7 2.2 fusion.76
  469.0 2.7 collective-permute-start.11
  481.8 2.2 fusion.60
  484.0 5.3 collective-permute-start.17
  499.4 2.2 fusion.68
  512.7 2.3 fusion.52
  517.0 9.2 %add_convert_fusion = bf16[2,2,256,512]{3,2,0,1:T(8,128)(2,1)S(1)} fusion(f32[2,256,512]{2,1,0:T(8,128)} %get-tuple-element.48, f32[2,256,512]{2,1,0:T(8,128)S(1)} %copy-done.14, f32[2,256,512]{2,1,0:T(8,128)} %get-tuple-element.69, f32[2,256,512]{2,1,0:T(8,128)S(1)} %copy-done.13, f32[2,256,512]{2,1,0:T(8,128)} %get-tuple-element.47, ...), kind=kLoop, calls=%fused_computation.2 | loop fusion | flops 20971520 | bytes 42991616 | tf_op jit(solution)/shard_map/convert_element_type | solution.py:151
  526.2 9.5 %add_convert_fusion.1 = bf16[2,2,256,512]{3,2,0,1:T(8,128)(2,1)S(1)} fusion(f32[2,256,512]{2,1,0:T(8,128)} %get-tuple-element.48, f32[2,256,512]{2,1,0:T(8,128)S(1)} %copy-done.14, f32[2,256,512]{2,1,0:T(8,128)} %get-tuple-element.69, f32[2,256,512]{2,1,0:T(8,128)S(1)} %copy-done.13, f32[2,256,512]{2,1,0:T(8,128)} %get-tuple-element.47, ...), kind=kLoop, calls=%fused_computation.3 | loop fusion | flops 20971520 | bytes 42991616 | tf_op jit(solution)/shard_map/convert_element_type | solution.py:150
  540.1 56.5 %reduce-scatter.4.cloned.1.call-done = bf16[128,512]{1,0:T(8,128)(2,1)} async-done(((bf16[256,512]{1,0:T(8,128)(2,1)}), bf16[128,512]{1,0:T(8,128)(2,1)}) %reduce-scatter.4.cloned.1.call-update) | async-done | bytes 131088
  598.9 2.5 collective-permute-start.20
  601.4 4.6 collective-permute-done.20
  609.3 3.4 collective-permute-start.22
  612.8 4.0 collective-permute-done.22
  616.8 4.5 collective-permute-start.23
  621.2 5.9 collective-permute-done.23
  627.1 7.6 %collective-permute-start.24 = (bf16[2,2,2,64,128]{4,3,0,2,1:T(8,128)(2,1)S(1)}, bf16[2,2,2,64,128]{4,3,0,2,1:T(8,128)(2,1)S(1)}, u32[]{:S(2)}, u32[]{:S(2)}) collective-permute-start(bf16[2,2,2,64,128]{4,3,0,2,1:T(8,128)(2,1)S(1)} %collective-permute-done.23), channel_id=1, source_target_pairs={{0,16},{16,0},{2,18},{18,2},{4,20},{20,4},{6,22},{22,6},{8,24},{24... | collective-permute-start | bytes 393224 | tf_op jit(solution)/shard_map/ppermute | solution.py:17
  634.7 9.9 %collective-permute-done.24 = bf16[2,2,2,64,128]{4,3,0,2,1:T(8,128)(2,1)S(1)} collective-permute-done((bf16[2,2,2,64,128]{4,3,0,2,1:T(8,128)(2,1)S(1)}, bf16[2,2,2,64,128]{4,3,0,2,1:T(8,128)(2,1)S(1)}, u32[]{:S(2)}, u32[]{:S(2)}) %collective-permute-start.24) | collective-permute-done | bytes 131104 | tf_op jit(solution)/shard_map/ppermute | solution.py:17
  644.6 12.0 %collective-permute-start.25 = (bf16[2,2,2,64,128]{4,3,0,2,1:T(8,128)(2,1)S(1)}, bf16[2,2,2,64,128]{4,3,0,2,1:T(8,128)(2,1)S(1)}, u32[]{:S(2)}, u32[]{:S(2)}) collective-permute-start(bf16[2,2,2,64,128]{4,3,0,2,1:T(8,128)(2,1)S(1)} %collective-permute-done.24), channel_id=1, source_target_pairs={{0,32},{32,0},{2,34},{34,2},{4,36},{36,4},{6,38},{38,6},{8,40},{40... | collective-permute-start | bytes 393224 | tf_op jit(solution)/shard_map/ppermute | solution.py:17
  656.6 12.1 %collective-permute-done.25 = bf16[2,2,2,64,128]{4,3,0,2,1:T(8,128)(2,1)S(1)} collective-permute-done((bf16[2,2,2,64,128]{4,3,0,2,1:T(8,128)(2,1)S(1)}, bf16[2,2,2,64,128]{4,3,0,2,1:T(8,128)(2,1)S(1)}, u32[]{:S(2)}, u32[]{:S(2)}) %collective-permute-start.25) | collective-permute-done | bytes 131104 | tf_op jit(solution)/shard_map/ppermute | solution.py:17
  668.7 2.4 collective-permute-start.26
  671.1 4.4 collective-permute-done.26
  675.5 3.9 collective-permute-start.27
  679.4 4.5 collective-permute-done.27
  (254 shorter events, 109.3 us)
Async XLA Ops:
  6.5 221.3 %copy-start = (f32[512,256]{1,0:T(8,128)S(1)}, f32[512,256]{1,0:T(8,128)}, u32[]{:S(2)}) copy-start(f32[512,256]{1,0:T(8,128)} %param.13) | copy-start | bytes 1572868
  6.5 590.1 %reduce-scatter.4.cloned.1.call-start = ((), (), s32[]{:S(2)}) async-start(), calls=%async_computation.1 | async-start | bytes 393216
  6.5 198.0 %collective-permute-start.9 = (bf16[2,2,256,256]{3,2,1,0:T(8,128)(2,1)}, bf16[2,2,256,256]{3,2,1,0:T(8,128)(2,1)}, u32[]{:S(2)}, u32[]{:S(2)}) collective-permute-start(bf16[2,2,256,256]{3,2,1,0:T(8,128)(2,1)} %param.9), channel_id=1, source_target_pairs={{0,2},{2,4},{4,6},{6,8},{8,10},{10,12},{12,14},{14,16},{16,18},{18... | collective-permute-start | bytes 1572872 | tf_op jit(solution)/shard_map/ppermute | solution.py:22
  8.6 197.9 %collective-permute-start.15 = (bf16[2,2,256,256]{3,2,1,0:T(8,128)(2,1)}, bf16[2,2,256,256]{3,2,1,0:T(8,128)(2,1)}, u32[]{:S(2)}, u32[]{:S(2)}) collective-permute-start(bf16[2,2,256,256]{3,2,1,0:T(8,128)(2,1)} %param.9), channel_id=1, source_target_pairs={{0,254},{2,0},{4,2},{6,4},{8,6},{10,8},{12,10},{14,12},{16,14},{18... | collective-permute-start | bytes 1572872 | tf_op jit(solution)/shard_map/ppermute | solution.py:22
  19.4 177.3 %collective-permute-start.10 = (bf16[2,2,64,512]{3,2,1,0:T(8,128)(2,1)}, bf16[2,2,64,512]{3,2,1,0:T(8,128)(2,1)}, u32[]{:S(2)}, u32[]{:S(2)}) collective-permute-start(bf16[2,2,64,512]{3,2,1,0:T(8,128)(2,1)} %param.10), channel_id=1, source_target_pairs={{0,2},{2,4},{4,6},{6,8},{8,10},{10,12},{12,14},{14,16},{16,18},{18... | collective-permute-start | bytes 786440 | tf_op jit(solution)/shard_map/ppermute | solution.py:22
  21.3 177.4 %collective-permute-start.16 = (bf16[2,2,64,512]{3,2,1,0:T(8,128)(2,1)}, bf16[2,2,64,512]{3,2,1,0:T(8,128)(2,1)}, u32[]{:S(2)}, u32[]{:S(2)}) collective-permute-start(bf16[2,2,64,512]{3,2,1,0:T(8,128)(2,1)} %param.10), channel_id=1, source_target_pairs={{0,254},{2,0},{4,2},{6,4},{8,6},{10,8},{12,10},{14,12},{16,14},{18... | collective-permute-start | bytes 786440 | tf_op jit(solution)/shard_map/ppermute | solution.py:22
  28.1 40.2 %collective-permute-start = (bf16[2,2,2,64,256]{4,3,0,2,1:T(8,128)(2,1)S(1)}, bf16[2,2,2,64,256]{4,3,0,2,1:T(8,128)(2,1)S(1)}, u32[]{:S(2)}, u32[]{:S(2)}) collective-permute-start(bf16[2,2,2,64,256]{4,3,0,2,1:T(8,128)(2,1)S(1)} %bitcast.651), channel_id=1, source_target_pairs={{0,256},{256,0},{1,257},{257,1},{2,258},{258,2},{3,259},{259,3},{4... | collective-permute-start | bytes 786440 | tf_op jit(solution)/shard_map/ppermute | solution.py:17
  59.0 3.0 copy-start.53
  66.1 4.2 copy-start.51
  68.3 6.3 copy-start.50
  68.3 8.3 %copy-start.55 = (bf16[2,2,2,64,256]{4,3,0,2,1:T(8,128)(2,1)}, bf16[2,2,2,64,256]{4,3,0,2,1:T(8,128)(2,1)S(1)}, u32[]{:S(2)}) copy-start(bf16[2,2,2,64,256]{4,3,0,2,1:T(8,128)(2,1)S(1)} %collective-permute-done) | copy-start | bytes 786436
  68.3 4.2 collective-permute-start.1
  72.5 12.6 %copy-start.49 = (bf16[2,2,256,512]{3,1,2,0:T(2,128)(2,1)S(1)}, bf16[2,2,256,512]{3,1,2,0:T(2,128)(2,1)}, u32[]{:S(2)}) copy-start(bf16[2,2,256,512]{3,1,2,0:T(2,128)(2,1)} %fusion.18) | copy-start | bytes 3145732
  72.5 10.7 %collective-permute-start.2 = (bf16[2,2,2,64,256]{4,3,0,2,1:T(8,128)(2,1)S(1)}, bf16[2,2,2,64,256]{4,3,0,2,1:T(8,128)(2,1)S(1)}, u32[]{:S(2)}, u32[]{:S(2)}) collective-permute-start(bf16[2,2,2,64,256]{4,3,0,2,1:T(8,128)(2,1)S(1)} %collective-permute-done.1), channel_id=1, source_target_pairs={{0,4},{4,0},{2,6},{6,2},{8,12},{12,8},{10,14},{14,10},{16,20},{20,... | collective-permute-start | bytes 786440 | tf_op jit(solution)/shard_map/ppermute | solution.py:17
  76.6 25.3 %copy-start.48 = (bf16[2,2,256,512]{3,1,2,0:T(2,128)(2,1)S(1)}, bf16[2,2,256,512]{3,1,2,0:T(2,128)(2,1)}, u32[]{:S(2)}) copy-start(bf16[2,2,256,512]{3,1,2,0:T(2,128)(2,1)} %fusion.19) | copy-start | bytes 3145732
  83.2 16.3 %collective-permute-start.3 = (bf16[2,2,2,64,256]{4,3,0,2,1:T(8,128)(2,1)S(1)}, bf16[2,2,2,64,256]{4,3,0,2,1:T(8,128)(2,1)S(1)}, u32[]{:S(2)}, u32[]{:S(2)}) collective-permute-start(bf16[2,2,2,64,256]{4,3,0,2,1:T(8,128)(2,1)S(1)} %collective-permute-done.2), channel_id=1, source_target_pairs={{0,8},{8,0},{2,10},{10,2},{4,12},{12,4},{6,14},{14,6},{16,24},{24,... | collective-permute-start | bytes 786440 | tf_op jit(solution)/shard_map/ppermute | solution.py:17
  87.1 54.1 %copy-start.47 = (bf16[2,2,256,512]{3,1,2,0:T(2,128)(2,1)S(1)}, bf16[2,2,256,512]{3,1,2,0:T(2,128)(2,1)}, u32[]{:S(2)}) copy-start(bf16[2,2,256,512]{3,1,2,0:T(2,128)(2,1)} %fusion.10) | copy-start | bytes 3145732
  99.5 27.1 %collective-permute-start.4 = (bf16[2,2,2,64,256]{4,3,0,2,1:T(8,128)(2,1)S(1)}, bf16[2,2,2,64,256]{4,3,0,2,1:T(8,128)(2,1)S(1)}, u32[]{:S(2)}, u32[]{:S(2)}) collective-permute-start(bf16[2,2,2,64,256]{4,3,0,2,1:T(8,128)(2,1)S(1)} %collective-permute-done.3), channel_id=1, source_target_pairs={{0,16},{16,0},{2,18},{18,2},{4,20},{20,4},{6,22},{22,6},{8,24},{24... | collective-permute-start | bytes 786440 | tf_op jit(solution)/shard_map/ppermute | solution.py:17
  103.9 57.0 %copy-start.46 = (bf16[2,2,256,512]{3,1,2,0:T(2,128)(2,1)S(1)}, bf16[2,2,256,512]{3,1,2,0:T(2,128)(2,1)}, u32[]{:S(2)}) copy-start(bf16[2,2,256,512]{3,1,2,0:T(2,128)(2,1)} %fusion.11) | copy-start | bytes 3145732
  126.6 31.6 %collective-permute-start.5 = (bf16[2,2,2,64,256]{4,3,0,2,1:T(8,128)(2,1)S(1)}, bf16[2,2,2,64,256]{4,3,0,2,1:T(8,128)(2,1)S(1)}, u32[]{:S(2)}, u32[]{:S(2)}) collective-permute-start(bf16[2,2,2,64,256]{4,3,0,2,1:T(8,128)(2,1)S(1)} %collective-permute-done.4), channel_id=1, source_target_pairs={{0,32},{32,0},{2,34},{34,2},{4,36},{36,4},{6,38},{38,6},{8,40},{40... | collective-permute-start | bytes 786440 | tf_op jit(solution)/shard_map/ppermute | solution.py:17
  143.3 29.3 %copy-start.59 = (s32[2]{0:T(128)S(1)}, s32[2]{0:T(128)}, u32[]{:S(2)}) copy-start(s32[2]{0:T(128)} %param.14) | copy-start | bytes 28
  158.2 10.2 %collective-permute-start.6 = (bf16[2,2,2,64,256]{4,3,0,2,1:T(8,128)(2,1)S(1)}, bf16[2,2,2,64,256]{4,3,0,2,1:T(8,128)(2,1)}, u32[]{:S(2)}, u32[]{:S(2)}) collective-permute-start(bf16[2,2,2,64,256]{4,3,0,2,1:T(8,128)(2,1)S(1)} %collective-permute-done.5), channel_id=1, source_target_pairs={{0,64},{64,0},{2,66},{66,2},{4,68},{68,4},{6,70},{70,6},{8,72},{72... | collective-permute-start | bytes 786440 | tf_op jit(solution)/shard_map/ppermute | solution.py:17
  168.4 43.8 %collective-permute-start.7 = (bf16[2,2,2,64,256]{4,3,0,2,1:T(8,128)(2,1)}, bf16[2,2,2,64,256]{4,3,0,2,1:T(8,128)(2,1)}, u32[]{:S(2)}, u32[]{:S(2)}) collective-permute-start(bf16[2,2,2,64,256]{4,3,0,2,1:T(8,128)(2,1)} %collective-permute-done.6), channel_id=1, source_target_pairs={{0,128},{128,0},{2,130},{130,2},{4,132},{132,4},{6,134},{134,6},{8... | collective-permute-start | bytes 786440 | tf_op jit(solution)/shard_map/ppermute | solution.py:17
  172.9 2.7 copy-start.29
  196.7 22.3 %copy-start.21 = (bf16[2,2,256,256]{3,2,1,0:T(8,128)(2,1)S(1)}, bf16[2,2,256,256]{3,2,1,0:T(8,128)(2,1)}, u32[]{:S(2)}) copy-start(bf16[2,2,256,256]{3,2,1,0:T(8,128)(2,1)} %param.9) | copy-start | bytes 1572868
  196.7 297.1 %collective-permute-start.13 = (bf16[2,2,64,512]{3,2,1,0:T(8,128)(2,1)}, bf16[2,2,64,512]{3,2,1,0:T(8,128)(2,1)}, u32[]{:S(2)}, u32[]{:S(2)}) collective-permute-start(bf16[2,2,64,512]{3,2,1,0:T(8,128)(2,1)} %collective-permute-done.10), channel_id=1, source_target_pairs={{0,2},{2,4},{4,6},{6,8},{8,10},{10,12},{12,14},{14,16},{16,18},{18... | collective-permute-start | bytes 786440 | tf_op jit(solution)/shard_map/ppermute | solution.py:22
  198.8 307.6 %collective-permute-start.19 = (bf16[2,2,64,512]{3,2,1,0:T(8,128)(2,1)}, bf16[2,2,64,512]{3,2,1,0:T(8,128)(2,1)}, u32[]{:S(2)}, u32[]{:S(2)}) collective-permute-start(bf16[2,2,64,512]{3,2,1,0:T(8,128)(2,1)} %collective-permute-done.16), channel_id=1, source_target_pairs={{0,254},{2,0},{4,2},{6,4},{8,6},{10,8},{12,10},{14,12},{16,14},{18... | collective-permute-start | bytes 786440 | tf_op jit(solution)/shard_map/ppermute | solution.py:22
  204.5 279.5 %collective-permute-start.12 = (bf16[2,2,256,256]{3,2,1,0:T(8,128)(2,1)}, bf16[2,2,256,256]{3,2,1,0:T(8,128)(2,1)}, u32[]{:S(2)}, u32[]{:S(2)}) collective-permute-start(bf16[2,2,256,256]{3,2,1,0:T(8,128)(2,1)} %collective-permute-done.9), channel_id=1, source_target_pairs={{0,2},{2,4},{4,6},{6,8},{8,10},{10,12},{12,14},{14,16},{16,18},{18... | collective-permute-start | bytes 1572872 | tf_op jit(solution)/shard_map/ppermute | solution.py:22
  206.5 295.2 %collective-permute-start.18 = (bf16[2,2,256,256]{3,2,1,0:T(8,128)(2,1)}, bf16[2,2,256,256]{3,2,1,0:T(8,128)(2,1)}, u32[]{:S(2)}, u32[]{:S(2)}) collective-permute-start(bf16[2,2,256,256]{3,2,1,0:T(8,128)(2,1)} %collective-permute-done.15), channel_id=1, source_target_pairs={{0,254},{2,0},{4,2},{6,4},{8,6},{10,8},{12,10},{14,12},{16,14},{18... | collective-permute-start | bytes 1572872 | tf_op jit(solution)/shard_map/ppermute | solution.py:22
  219.0 7.1 %copy-start.56 = (f32[256,2,64]{0,2,1:T(8,128)S(1)}, f32[256,2,64]{0,2,1:T(8,128)}, u32[]{:S(2)}) copy-start(f32[256,2,64]{0,2,1:T(8,128)} %get-tuple-element.54) | copy-start | bytes 393220
  219.0 7.1 %copy-start.57 = (f32[256,2,64]{0,2,1:T(8,128)S(1)}, f32[256,2,64]{0,2,1:T(8,128)}, u32[]{:S(2)}) copy-start(f32[256,2,64]{0,2,1:T(8,128)} %get-tuple-element.55) | copy-start | bytes 393220
  221.3 233.1 %collective-permute-start.8 = (bf16[2,2,2,64,256]{4,3,0,2,1:T(8,128)(2,1)}, bf16[2,2,2,64,256]{4,3,0,2,1:T(8,128)(2,1)}, u32[]{:S(2)}, u32[]{:S(2)}) collective-permute-start(bf16[2,2,2,64,256]{4,3,0,2,1:T(8,128)(2,1)} %fusion.89), channel_id=1, source_target_pairs={{0,2},{2,4},{4,6},{6,8},{8,10},{10,12},{12,14},{14,16},{16,18},{18... | collective-permute-start | bytes 786440 | tf_op jit(solution)/shard_map/ppermute | solution.py:22
  228.4 223.1 %copy-start.45 = (bf16[2,2,64,256]{3,2,1,0:T(8,128)(2,1)S(1)}, bf16[2,2,64,256]{3,2,1,0:T(8,128)(2,1)}, u32[]{:S(2)}) copy-start(bf16[2,2,64,256]{3,2,1,0:T(8,128)(2,1)} %get-tuple-element.66) | copy-start | bytes 393220
  454.4 60.6 %copy-start.20 = (f32[2,256,512]{2,1,0:T(8,128)}, f32[2,256,512]{2,1,0:T(8,128)S(1)}, u32[]{:S(2)}) copy-start(f32[2,256,512]{2,1,0:T(8,128)S(1)} %get-tuple-element.15) | copy-start | bytes 3145732
  454.4 14.6 %collective-permute-start.14 = (bf16[2,2,2,64,256]{4,3,0,2,1:T(8,128)(2,1)}, bf16[2,2,2,64,256]{4,3,0,2,1:T(8,128)(2,1)S(1)}, u32[]{:S(2)}, u32[]{:S(2)}) collective-permute-start(bf16[2,2,2,64,256]{4,3,0,2,1:T(8,128)(2,1)} %fusion.89), channel_id=1, source_target_pairs={{0,254},{2,0},{4,2},{6,4},{8,6},{10,8},{12,10},{14,12},{16,14},{18... | collective-permute-start | bytes 786440 | tf_op jit(solution)/shard_map/ppermute | solution.py:22
  469.0 20.3 %collective-permute-start.11 = (bf16[2,2,2,64,256]{4,3,0,2,1:T(8,128)(2,1)}, bf16[2,2,2,64,256]{4,3,0,2,1:T(8,128)(2,1)S(1)}, u32[]{:S(2)}, u32[]{:S(2)}) collective-permute-start(bf16[2,2,2,64,256]{4,3,0,2,1:T(8,128)(2,1)} %collective-permute-done.8), channel_id=1, source_target_pairs={{0,2},{2,4},{4,6},{6,8},{8,10},{10,12},{12,14},{14,16},{16,18},{18... | collective-permute-start | bytes 786440 | tf_op jit(solution)/shard_map/ppermute | solution.py:22
  484.0 17.6 %collective-permute-start.17 = (bf16[2,2,2,64,256]{4,3,0,2,1:T(8,128)(2,1)S(1)}, bf16[2,2,2,64,256]{4,3,0,2,1:T(8,128)(2,1)S(1)}, u32[]{:S(2)}, u32[]{:S(2)}) collective-permute-start(bf16[2,2,2,64,256]{4,3,0,2,1:T(8,128)(2,1)S(1)} %collective-permute-done.14), channel_id=1, source_target_pairs={{0,254},{2,0},{4,2},{6,4},{8,6},{10,8},{12,10},{14,12},{16,14},{18... | collective-permute-start | bytes 786440 | tf_op jit(solution)/shard_map/ppermute | solution.py:22
  503.9 11.0 %copy-start.19 = (f32[2,256,512]{2,1,0:T(8,128)S(1)}, f32[2,256,512]{2,1,0:T(8,128)}, u32[]{:S(2)}) copy-start(f32[2,256,512]{2,1,0:T(8,128)} %copy.99) | copy-start | bytes 3145732
  506.3 8.6 %copy-start.16 = (f32[2,256,512]{2,1,0:T(8,128)S(1)}, f32[2,256,512]{2,1,0:T(8,128)}, u32[]{:S(2)}) copy-start(f32[2,256,512]{2,1,0:T(8,128)} %copy.93) | copy-start | bytes 3145732
  506.3 8.6 %copy-start.17 = (f32[2,256,512]{2,1,0:T(8,128)S(1)}, f32[2,256,512]{2,1,0:T(8,128)}, u32[]{:S(2)}) copy-start(f32[2,256,512]{2,1,0:T(8,128)} %copy.95) | copy-start | bytes 3145732
  506.3 8.6 %copy-start.18 = (f32[2,256,512]{2,1,0:T(8,128)S(1)}, f32[2,256,512]{2,1,0:T(8,128)}, u32[]{:S(2)}) copy-start(f32[2,256,512]{2,1,0:T(8,128)} %copy.96) | copy-start | bytes 3145732
  507.9 7.1 %copy-start.14 = (f32[2,256,512]{2,1,0:T(8,128)S(1)}, f32[2,256,512]{2,1,0:T(8,128)}, u32[]{:S(2)}) copy-start(f32[2,256,512]{2,1,0:T(8,128)} %copy.124) | copy-start | bytes 3145732
  507.9 7.1 %copy-start.15 = (f32[2,256,512]{2,1,0:T(8,128)S(1)}, f32[2,256,512]{2,1,0:T(8,128)}, u32[]{:S(2)}) copy-start(f32[2,256,512]{2,1,0:T(8,128)} %copy.92) | copy-start | bytes 3145732
  509.5 5.5 copy-start.11
  509.5 5.5 copy-start.12
  509.5 5.5 copy-start.13
  511.0 4.0 copy-start.8
  511.0 4.0 copy-start.9
  511.0 4.0 copy-start.10
  512.6 2.7 copy-start.3
  512.6 3.5 copy-start.4
  512.6 3.7 copy-start.5
  512.6 4.0 copy-start.6
  512.7 4.3 copy-start.7
  538.3 59.6 %copy-start.58 = (f32[2,64,128]{2,1,0:T(8,128)S(1)}, f32[2,64,128]{2,1,0:T(8,128)}, u32[]{:S(2)}) copy-start(f32[2,64,128]{2,1,0:T(8,128)} %param.11) | copy-start | bytes 196612
  539.1 146.2 %copy-start.1 = (f32[512,256]{1,0:T(8,128)S(1)}, f32[512,256]{1,0:T(8,128)}, u32[]{:S(2)}) copy-start(f32[512,256]{1,0:T(8,128)} %param.13) | copy-start | bytes 1572868
  598.9 7.1 %collective-permute-start.20 = (bf16[2,2,2,64,128]{4,3,0,2,1:T(8,128)(2,1)S(1)}, bf16[2,2,2,64,128]{4,3,0,2,1:T(8,128)(2,1)S(1)}, u32[]{:S(2)}, u32[]{:S(2)}) collective-permute-start(bf16[2,2,2,64,128]{4,3,0,2,1:T(8,128)(2,1)S(1)} %add_convert_fusion.7), channel_id=1, source_target_pairs={{0,256},{256,0},{1,257},{257,1},{2,258},{258,2},{3,259},{259,3},{4... | collective-permute-start | bytes 393224 | tf_op jit(solution)/shard_map/ppermute | solution.py:17
  606.1 3.2 collective-permute-start.21
  609.3 7.4 %collective-permute-start.22 = (bf16[2,2,2,64,128]{4,3,0,2,1:T(8,128)(2,1)S(1)}, bf16[2,2,2,64,128]{4,3,0,2,1:T(8,128)(2,1)S(1)}, u32[]{:S(2)}, u32[]{:S(2)}) collective-permute-start(bf16[2,2,2,64,128]{4,3,0,2,1:T(8,128)(2,1)S(1)} %collective-permute-done.21), channel_id=1, source_target_pairs={{0,4},{4,0},{2,6},{6,2},{8,12},{12,8},{10,14},{14,10},{16,20},{20,... | collective-permute-start | bytes 393224 | tf_op jit(solution)/shard_map/ppermute | solution.py:17
  616.8 10.3 %collective-permute-start.23 = (bf16[2,2,2,64,128]{4,3,0,2,1:T(8,128)(2,1)S(1)}, bf16[2,2,2,64,128]{4,3,0,2,1:T(8,128)(2,1)S(1)}, u32[]{:S(2)}, u32[]{:S(2)}) collective-permute-start(bf16[2,2,2,64,128]{4,3,0,2,1:T(8,128)(2,1)S(1)} %collective-permute-done.22), channel_id=1, source_target_pairs={{0,8},{8,0},{2,10},{10,2},{4,12},{12,4},{6,14},{14,6},{16,24},{24,... | collective-permute-start | bytes 393224 | tf_op jit(solution)/shard_map/ppermute | solution.py:17
  627.1 17.5 %collective-permute-start.24 = (bf16[2,2,2,64,128]{4,3,0,2,1:T(8,128)(2,1)S(1)}, bf16[2,2,2,64,128]{4,3,0,2,1:T(8,128)(2,1)S(1)}, u32[]{:S(2)}, u32[]{:S(2)}) collective-permute-start(bf16[2,2,2,64,128]{4,3,0,2,1:T(8,128)(2,1)S(1)} %collective-permute-done.23), channel_id=1, source_target_pairs={{0,16},{16,0},{2,18},{18,2},{4,20},{20,4},{6,22},{22,6},{8,24},{24... | collective-permute-start | bytes 393224 | tf_op jit(solution)/shard_map/ppermute | solution.py:17
  644.6 24.1 %collective-permute-start.25 = (bf16[2,2,2,64,128]{4,3,0,2,1:T(8,128)(2,1)S(1)}, bf16[2,2,2,64,128]{4,3,0,2,1:T(8,128)(2,1)S(1)}, u32[]{:S(2)}, u32[]{:S(2)}) collective-permute-start(bf16[2,2,2,64,128]{4,3,0,2,1:T(8,128)(2,1)S(1)} %collective-permute-done.24), channel_id=1, source_target_pairs={{0,32},{32,0},{2,34},{34,2},{4,36},{36,4},{6,38},{38,6},{8,40},{40... | collective-permute-start | bytes 393224 | tf_op jit(solution)/shard_map/ppermute | solution.py:17
  668.7 6.8 collective-permute-start.26
  675.5 8.4 %collective-permute-start.27 = (bf16[2,2,2,64,128]{4,3,0,2,1:T(8,128)(2,1)S(1)}, bf16[2,2,2,64,128]{4,3,0,2,1:T(8,128)(2,1)S(1)}, u32[]{:S(2)}, u32[]{:S(2)}) collective-permute-start(bf16[2,2,2,64,128]{4,3,0,2,1:T(8,128)(2,1)S(1)} %collective-permute-done.26), channel_id=1, source_target_pairs={{0,128},{128,0},{2,130},{130,2},{4,132},{132,4},{6,134},{134,6},{8... | collective-permute-start | bytes 393224 | tf_op jit(solution)/shard_map/ppermute | solution.py:17
  (25 other events, 54.5 us)
Sparse Core Ops, SparseCore 0:
  540.2 56.3 reduce-scatter.3
